TPU v7x, 512 devices: a whole 4x4x16 slice. The times are simulated.
512 devices in a mesh: node: 32 (over z, core), local: 16 (over y, x).
Axes of the slice: x: 4, y: 4, z: 16, core: 2. Of those that a mesh axis runs over, the one named last changes fastest.
Arguments:
- images: float32 [4096, 7, 7, 512], P(('node', 'local')), may hold values from -11 to 11, as said below
- targets: float32 [4096, 7, 7, 512], P(('node', 'local')), may hold values from -6 to 6
- weight: float32 [3, 3, 512, 512], replicated, may hold values from -0.09375 to 0.09375
Outputs:
- combined: float32 [4608, 512], P('local', 'node')
Inputs may be any that keep to these rules, and one draw needn't show every extreme that they name: `images`: entries are real-valued, of order one.
All inputs are finite; a program needn't handle non-finite values.
Results may differ from a plain program's by a relative error of at most 0.00013.
Values sent between devices are 32-bit elements; how exact they have to be, the bound alone decides.
A program may use at most 128 MiB of HBM per device.

v0:
```python
import jax
import jax.numpy as jnp
from jax import lax
from jax.sharding import PartitionSpec as P

SIDE = 7


epsilon = 1e-06


def partner(value, axis, distance):
    mask = 2**distance
    pairs = [(source, source ^ mask) for source in range(lax.axis_size(axis))]
    return lax.ppermute(value, axis, pairs)


def make_patches(images):
    padded = jnp.pad(images, ((0, 0), (1, 1), (1, 1), (0, 0)))
    tap_views = []
    for row_shift in range(3):
        for col_shift in range(3):
            tap_views.append(
                padded[:, row_shift : row_shift + SIDE, col_shift : col_shift + SIDE, :]
            )
    joined = jnp.concatenate(tap_views, axis=-1)
    return joined.reshape(-1, 9 * images.shape[3])


def adasum_pair(left_vec, right_vec, cross_sum, left_sq, right_sq):
    left_coef = 1.0 - cross_sum / (2.0 * (left_sq + epsilon))
    right_coef = 1.0 - cross_sum / (2.0 * (right_sq + epsilon))
    return left_coef * left_vec + right_coef * right_vec


def on_device(images, targets, weight):
    channels = images.shape[3]
    flat_w = weight.reshape(9 * channels, channels)
    patches = make_patches(images)
    outputs = jnp.dot(
        patches, flat_w, precision=lax.Precision.HIGHEST, preferred_element_type=jnp.float32
    )
    residual = outputs - targets.reshape(-1, channels)
    row_scale = 1.0 / patches.shape[0]
    product = lax.dot_general(
        patches,
        residual,
        (((0,), (0,)), ((), ())),
        precision=lax.Precision.HIGHEST,
        preferred_element_type=jnp.float32,
    )
    my_rows = lax.psum_scatter(product * row_scale, "local", scatter_dimension=0, tiled=True)
    node_count = lax.axis_size("node")
    levels = node_count.bit_length() - 1
    col_width = channels // node_count
    node_id = lax.axis_index("node")
    merged = my_rows
    for tree_level in range(levels):
        opposite = partner(merged, "node", tree_level)
        pair_sums = lax.psum(
            (jnp.sum(merged * opposite), jnp.sum(merged * merged), jnp.sum(opposite * opposite)),
            "local",
        )
        merged = adasum_pair(merged, opposite, pair_sums[0], pair_sums[1], pair_sums[2])
    return lax.dynamic_slice_in_dim(merged, node_id * col_width, col_width, 1)


def solution(mesh):
    return jax.shard_map(
        on_device,
        mesh=mesh,
        in_specs=(
            P(("node", "local"), None, None, None),
            P(("node", "local"), None, None, None),
            P(),
        ),
        out_specs=P("local", "node"),
        check_vma=False,
    )
```

profile of v0, /device:TPU:96, one launch (start us, length us, event | category | flops | bytes accessed | tf_op | source)
XLA Modules:
  0.0 498.3 jit_solution(8646347275590807067)
XLA Ops:
  6.5 0.0 copy-start
  6.5 0.0 reduce-scatter.2.cloned.1.call-start
  6.5 1.2 fusion
  7.8 1.2 fusion.1
  9.0 1.1 fusion.2
  10.1 1.2 fusion.3
  11.3 1.2 constant_dynamic-update-slice_fusion
  12.5 0.0 copy-done
  12.5 0.1 fusion.4
  12.6 0.1 fusion.5
  12.7 0.1 fusion.6
  12.7 0.1 fusion.7
  12.8 7.4 %copy.5 = f32[8,7,7,4608]{3,2,1,0:T(8,128)} copy(f32[8,7,7,4608]{3,0,2,1:T(8,128)S(1)} %fusion.7) | data formatting | bytes 14450688 | tf_op jit(solution)/shard_map/concatenate | solution.py:26
  20.3 0.0 copy-start.1
  20.3 9.1 %reshape.9 = f32[392,4608]{1,0:T(8,128)} reshape(f32[8,7,7,4608]{3,2,1,0:T(8,128)} %copy.5) | data formatting | bytes 14450688 | tf_op jit(solution)/shard_map/reshape | solution.py:27
  29.4 0.0 copy-done.1
  29.4 1.4 copy.6
  30.8 0.0 slice-start
  30.8 2.3 reshape.11
  33.1 0.0 slice-start.1
  33.1 15.3 %convolution_subtract_fusion = f32[392,512]{1,0:T(8,128)S(1)} fusion(f32[392,512]{1,0:T(8,128)} %reshape.11, f32[392,4608]{1,0:T(8,128)} %reshape.9, f32[4608,512]{1,0:T(8,128)} %bitcast.7), kind=kOutput, calls=%fused_computation.9 | convolution fusion | flops 11098329088 | bytes 18268160 | tf_op jit(solution)/shard_map/dot_general | solution.py:40
  48.4 0.0 slice-done
  48.4 0.0 slice-done.1
  48.4 18.0 %convolution_multiply_fusion = f32[4608,512]{1,0:T(8,128)} fusion(f32[392,4608]{1,0:T(8,128)S(1)} %bitcast.6, f32[392,512]{1,0:T(8,128)S(1)} %convolution_subtract_fusion), kind=kOutput, calls=%fused_computation | convolution fusion | flops 11100487680 | bytes 17465344 | tf_op jit(solution)/shard_map/dot_general | solution.py:45
  66.4 0.0 reduce-scatter.2.cloned.1.call-update
  66.4 106.3 %reduce-scatter.2.cloned.1.call-done = f32[288,512]{1,0:T(8,128)} async-done(((f32[4608,512]{1,0:T(8,128)}), f32[288,512]{1,0:T(8,128)}) %reduce-scatter.2.cloned.1.call-update) | async-done | bytes 589840 | tf_op jit(solution)/shard_map/reduce_scatter | solution.py:52
  172.8 1.9 collective-permute-start
  174.7 2.2 collective-permute-done
  176.9 1.9 multiply_reduce_fusion.13
  178.8 38.8 %all-reduce.5 = (f32[]{:T(128)}, f32[]{:T(128)}, f32[]{:T(128)}) all-reduce(f32[]{:T(128)} %get-tuple-element.18, f32[]{:T(128)} %get-tuple-element.19, f32[]{:T(128)} %get-tuple-element.17), channel_id=1, replica_groups=mesh['node'=32,'local'=16] {'local'}, use_global_device_ids=true, to_apply=%region_2.3 | all-reduce | flops 3 | bytes 24 | tf_op jit(solution)/shard_map/psum | solution.py:60
  220.1 1.2 multiply_add_fusion.3
  221.3 2.4 collective-permute-start.1
  223.7 9.4 %collective-permute-done.1 = f32[288,512]{1,0:T(8,128)S(1)} collective-permute-done((f32[288,512]{1,0:T(8,128)S(1)}, f32[288,512]{1,0:T(8,128)S(1)}, u32[]{:S(2)}, u32[]{:S(2)}) %collective-permute-start.1) | collective-permute-done | bytes 589856 | tf_op jit(solution)/shard_map/ppermute | solution.py:15
  233.1 0.9 multiply_reduce_fusion.10
  234.0 36.1 %all-reduce.4 = (f32[]{:T(128)}, f32[]{:T(128)}, f32[]{:T(128)}) all-reduce(f32[]{:T(128)} %get-tuple-element.15, f32[]{:T(128)} %get-tuple-element.16, f32[]{:T(128)} %get-tuple-element.14), channel_id=1, replica_groups=mesh['node'=32,'local'=16] {'local'}, use_global_device_ids=true, to_apply=%region_8.9 | all-reduce | flops 3 | bytes 24 | tf_op jit(solution)/shard_map/psum | solution.py:60
  272.7 0.1 multiply_add_fusion.2
  272.8 2.3 collective-permute-start.2
  275.1 16.6 %collective-permute-done.2 = f32[288,512]{1,0:T(8,128)S(1)} collective-permute-done((f32[288,512]{1,0:T(8,128)S(1)}, f32[288,512]{1,0:T(8,128)S(1)}, u32[]{:S(2)}, u32[]{:S(2)}) %collective-permute-start.2) | collective-permute-done | bytes 589856 | tf_op jit(solution)/shard_map/ppermute | solution.py:15
  291.7 0.9 multiply_reduce_fusion.7
  292.6 38.1 %all-reduce.3 = (f32[]{:T(128)}, f32[]{:T(128)}, f32[]{:T(128)}) all-reduce(f32[]{:T(128)} %get-tuple-element.12, f32[]{:T(128)} %get-tuple-element.13, f32[]{:T(128)} %get-tuple-element.11), channel_id=1, replica_groups=mesh['node'=32,'local'=16] {'local'}, use_global_device_ids=true, to_apply=%region_14.15 | all-reduce | flops 3 | bytes 24 | tf_op jit(solution)/shard_map/psum | solution.py:60
  333.3 0.1 multiply_add_fusion.1
  333.5 7.6 %collective-permute-start.3 = (f32[288,512]{1,0:T(8,128)S(1)}, f32[288,512]{1,0:T(8,128)S(1)}, u32[]{:S(2)}, u32[]{:S(2)}) collective-permute-start(f32[288,512]{1,0:T(8,128)S(1)} %multiply_add_fusion.1), channel_id=1, source_target_pairs={{0,128},{16,144},{32,160},{48,176},{64,192},{80,208},{96,224},{112... | collective-permute-start | bytes 1769480 | tf_op jit(solution)/shard_map/ppermute | solution.py:15
  341.1 24.7 %collective-permute-done.3 = f32[288,512]{1,0:T(8,128)S(1)} collective-permute-done((f32[288,512]{1,0:T(8,128)S(1)}, f32[288,512]{1,0:T(8,128)S(1)}, u32[]{:S(2)}, u32[]{:S(2)}) %collective-permute-start.3) | collective-permute-done | bytes 589856 | tf_op jit(solution)/shard_map/ppermute | solution.py:15
  365.8 0.9 multiply_reduce_fusion.4
  366.7 36.7 %all-reduce.2 = (f32[]{:T(128)}, f32[]{:T(128)}, f32[]{:T(128)}) all-reduce(f32[]{:T(128)} %get-tuple-element.9, f32[]{:T(128)} %get-tuple-element.10, f32[]{:T(128)} %get-tuple-element.8), channel_id=1, replica_groups=mesh['node'=32,'local'=16] {'local'}, use_global_device_ids=true, to_apply=%region_20.21 | all-reduce | flops 3 | bytes 24 | tf_op jit(solution)/shard_map/psum | solution.py:60
  406.0 0.1 multiply_add_fusion
  406.1 6.7 %collective-permute-start.4 = (f32[288,512]{1,0:T(8,128)S(1)}, f32[288,512]{1,0:T(8,128)S(1)}, u32[]{:S(2)}, u32[]{:S(2)}) collective-permute-start(f32[288,512]{1,0:T(8,128)S(1)} %multiply_add_fusion), channel_id=1, source_target_pairs={{0,256},{16,272},{32,288},{48,304},{64,320},{80,336},{96,352},{112... | collective-permute-start | bytes 1769480 | tf_op jit(solution)/shard_map/ppermute | solution.py:15
  412.8 36.7 %collective-permute-done.4 = f32[288,512]{1,0:T(8,128)S(1)} collective-permute-done((f32[288,512]{1,0:T(8,128)S(1)}, f32[288,512]{1,0:T(8,128)S(1)}, u32[]{:S(2)}, u32[]{:S(2)}) %collective-permute-start.4) | collective-permute-done | bytes 589856 | tf_op jit(solution)/shard_map/ppermute | solution.py:15
  449.5 0.9 multiply_reduce_fusion.1
  450.4 37.6 %all-reduce.1 = (f32[]{:T(128)}, f32[]{:T(128)}, f32[]{:T(128)}) all-reduce(f32[]{:T(128)} %get-tuple-element.6, f32[]{:T(128)} %get-tuple-element.7, f32[]{:T(128)} %get-tuple-element.5), channel_id=1, replica_groups=mesh['node'=32,'local'=16] {'local'}, use_global_device_ids=true, to_apply=%region_26.27 | all-reduce | flops 3 | bytes 24 | tf_op jit(solution)/shard_map/psum | solution.py:60
  490.6 0.1 fusion.8
  490.7 0.7 copy.7
  (1 shorter events, 0.0 us)
Async XLA Ops:
  6.5 6.0 %copy-start = (f32[8,7,7,512]{3,0,2,1:T(8,128)S(1)}, f32[8,7,7,512]{3,0,2,1:T(8,128)}, u32[]{:S(2)}) copy-start(f32[8,7,7,512]{3,0,2,1:T(8,128)} %param.3) | copy-start | bytes 2408452
  6.5 166.2 %reduce-scatter.2.cloned.1.call-start = ((), (), s32[]{:S(2)}) async-start(), calls=%async_computation.1 | async-start | bytes 10027008 | tf_op jit(solution)/shard_map/reduce_scatter | solution.py:52
  20.3 9.1 %copy-start.1 = (f32[8,7,7,512]{3,0,2,1:T(8,128)S(1)}, f32[8,7,7,512]{3,0,2,1:T(8,128)}, u32[]{:S(2)}) copy-start(f32[8,7,7,512]{3,0,2,1:T(8,128)} %param.4) | copy-start | bytes 2408452
  30.8 17.6 %slice-start = ((s8[7225344]{0:T(1024)(128)(4,1)}), s8[3031040]{0:T(1024)(128)(4,1)S(1)}, s32[]{:S(2)}) async-start(s8[7225344]{0:T(1024)(128)(4,1)} %bitcast.5), calls=%async_computation.2 | async-start | bytes 6062080
  33.1 15.3 %slice-start.1 = ((s8[7225344]{0:T(1024)(128)(4,1)}), s8[4194304]{0:T(1024)(128)(4,1)S(1)}, s32[]{:S(2)}) async-start(s8[7225344]{0:T(1024)(128)(4,1)} %bitcast.5), calls=%async_computation.3 | async-start | bytes 8388608
  172.8 4.1 collective-permute-start
  221.3 11.8 %collective-permute-start.1 = (f32[288,512]{1,0:T(8,128)S(1)}, f32[288,512]{1,0:T(8,128)S(1)}, u32[]{:S(2)}, u32[]{:S(2)}) collective-permute-start(f32[288,512]{1,0:T(8,128)S(1)} %multiply_add_fusion.3), channel_id=1, source_target_pairs={{0,32},{16,48},{32,0},{48,16},{64,96},{80,112},{96,64},{112,80},{1... | collective-permute-start | bytes 1769480 | tf_op jit(solution)/shard_map/ppermute | solution.py:15
  272.8 18.9 %collective-permute-start.2 = (f32[288,512]{1,0:T(8,128)S(1)}, f32[288,512]{1,0:T(8,128)S(1)}, u32[]{:S(2)}, u32[]{:S(2)}) collective-permute-start(f32[288,512]{1,0:T(8,128)S(1)} %multiply_add_fusion.2), channel_id=1, source_target_pairs={{0,64},{16,80},{32,96},{48,112},{64,0},{80,16},{96,32},{112,48},{1... | collective-permute-start | bytes 1769480 | tf_op jit(solution)/shard_map/ppermute | solution.py:15
  333.5 32.3 %collective-permute-start.3 = (f32[288,512]{1,0:T(8,128)S(1)}, f32[288,512]{1,0:T(8,128)S(1)}, u32[]{:S(2)}, u32[]{:S(2)}) collective-permute-start(f32[288,512]{1,0:T(8,128)S(1)} %multiply_add_fusion.1), channel_id=1, source_target_pairs={{0,128},{16,144},{32,160},{48,176},{64,192},{80,208},{96,224},{112... | collective-permute-start | bytes 1769480 | tf_op jit(solution)/shard_map/ppermute | solution.py:15
  406.1 43.4 %collective-permute-start.4 = (f32[288,512]{1,0:T(8,128)S(1)}, f32[288,512]{1,0:T(8,128)S(1)}, u32[]{:S(2)}, u32[]{:S(2)}) collective-permute-start(f32[288,512]{1,0:T(8,128)S(1)} %multiply_add_fusion), channel_id=1, source_target_pairs={{0,256},{16,272},{32,288},{48,304},{64,320},{80,336},{96,352},{112... | collective-permute-start | bytes 1769480 | tf_op jit(solution)/shard_map/ppermute | solution.py:15
Sparse Core Ops, SparseCore 0:
  66.6 106.1 reduce-scatter.1
where the time goes:
time: 499 us; the launch traced here: 498 us
  waiting for transfers between devices  196 us (39%)
  blocking collectives  187 us (37%)
  matrix products  33.2 us (7%)
  local copies, waits for them, and re-layouts  27.2 us (5%)
  between operations  26.4 us (5%)
  starting transfers between devices  21 us (4%)
  other arithmetic  7.13 us (1%)
    psum x5, blocking collectives, on_device(): lax.psum((jnp.sum(merged * opposite), jnp.sum(merged * merged), jnp.sum(o...  187 us
    reduce_scatter x1, waiting for transfers between devices, on_device(): lax.psum_scatter(product * row_scale, 'local', scatter_dimension=0, tiled...  106 us
    ppermute x5, waiting for transfers between devices, partner(): return lax.ppermute(value, axis, pairs)  89.5 us
    ppermute x5, starting transfers between devices, partner(): return lax.ppermute(value, axis, pairs)  21 us
    dot_general x1, matrix products, on_device(): lax.dot_general(patches, residual, (((0,), (0,)), ((), ())), precision=la...  18 us
    dot_general x1, matrix products, on_device(): jnp.dot(patches, flat_w, precision=lax.Precision.HIGHEST, preferred_eleme...  15.3 us
  transfers between devices with their start and end apart: 6, of which 6 were waited for; matrix products, arithmetic and copies ran while one was open for 0% of the time, Pallas kernels for 0%

commit v1 on v0

v1 whole, which is shorter than its diff:
```python
import jax
import jax.numpy as jnp
from jax import lax
from jax.sharding import PartitionSpec as P

SIDE = 7
EPS = 1e-06
HIGHEST = lax.Precision.HIGHEST


def make_patches(images):
    padded = jnp.pad(images, ((0, 0), (1, 1), (1, 1), (0, 0)))
    views = []
    for i in range(3):
        for j in range(3):
            views.append(padded[:, i : i + SIDE, j : j + SIDE, :])
    return jnp.concatenate(views, axis=-1).reshape(-1, 9 * images.shape[3])


def tree_coefs(gram):
    rows = jnp.eye(gram.shape[0], dtype=jnp.float32)
    while rows.shape[0] > 1:
        a, b = rows[0::2], rows[1::2]
        ga = jnp.dot(a, gram, precision=HIGHEST)
        gb = jnp.dot(b, gram, precision=HIGHEST)
        ab = jnp.sum(ga * b, axis=1, keepdims=True)
        aa = jnp.maximum(jnp.sum(ga * a, axis=1, keepdims=True), 0.0)
        bb = jnp.maximum(jnp.sum(gb * b, axis=1, keepdims=True), 0.0)
        rows = (1.0 - ab / (2.0 * (aa + EPS))) * a + (1.0 - ab / (2.0 * (bb + EPS))) * b
    return rows[0]


def on_device(images, targets, weight):
    channels = images.shape[3]
    nodes = lax.axis_size("node")
    flat_w = weight.reshape(9 * channels, channels)
    patches = make_patches(images)
    outputs = jnp.dot(patches, flat_w, precision=lax.Precision.HIGH, preferred_element_type=jnp.float32)
    residual = outputs - targets.reshape(-1, channels)
    product = lax.dot_general(
        patches, residual, (((0,), (0,)), ((), ())), precision=lax.Precision.HIGH, preferred_element_type=jnp.float32
    )
    mine = lax.psum_scatter(product * (1.0 / patches.shape[0]), "local", scatter_dimension=0, tiled=True)
    split = jnp.swapaxes(mine.reshape(-1, nodes, channels // nodes), 0, 1)
    blocks = lax.all_to_all(split, "node", 0, 0, tiled=True)
    flat = blocks.reshape(nodes, -1)
    gram = lax.psum(lax.dot_general(flat, flat, (((1,), (1,)), ((), ())), precision=HIGHEST), ("node", "local"))
    coefs = tree_coefs(gram)
    return jnp.sum(coefs[:, None, None] * blocks, axis=0)


def solution(mesh):
    image_spec = P(("node", "local"), None, None, None)
    return jax.shard_map(
        on_device, mesh=mesh, in_specs=(image_spec, image_spec, P()), out_specs=P("local", "node"), check_vma=False
    )
```

time: 499 us -> 339 us (0.68)
  the two profiles are of different devices: /device:TPU:96 before, /device:TPU:1 now
where the time goes in v1:
time: 339 us
  waiting for transfers between devices  152 us (45%)
  blocking collectives  99.5 us (29%)
  local copies, waits for them, and re-layouts  28.9 us (9%)
  matrix products  27.3 us (8%)
  between operations  16.2 us (5%)
  starting transfers between devices  14.2 us (4%)
    reduce_scatter x1, waiting for transfers between devices, on_device(): lax.psum_scatter(product * (1.0 / patches.shape[0]), 'local', scatter_dim...  107 us
    psum x1, blocking collectives, on_device(): lax.psum(lax.dot_general(flat, flat, (((1,), (1,)), ((), ())), precision=...  99.5 us
    all_to_all x1, waiting for transfers between devices, on_device(): blocks = lax.all_to_all(split, 'node', 0, 0, tiled=True)  44.5 us
    all_to_all x1, starting transfers between devices, on_device(): blocks = lax.all_to_all(split, 'node', 0, 0, tiled=True)  14.2 us
    dot_general x1, matrix products, on_device(): jnp.dot(patches, flat_w, precision=lax.Precision.HIGH, preferred_element_...  12.5 us
    dot_general x1, matrix products, on_device(): lax.dot_general(patches, residual, (((0,), (0,)), ((), ())), precision=la...  10.3 us
    reshape x1, local copies, waits for them, and re-layouts, make_patches(): return jnp.concatenate(views, axis=-1).reshape(-1, 9 * images.shape[3])  9.12 us
    unnamed x17, local copies, waits for them, and re-layouts  7.56 us
  transfers between devices with their start and end apart: 2, of which 2 were waited for; matrix products, arithmetic and copies ran while one was open for 0% of the time, Pallas kernels for 0%

profile of v1, /device:TPU:1, one launch (start us, length us, event | category | flops | bytes accessed | tf_op | source)
XLA Modules:
  0.0 338.8 jit_solution(9154490214921103050)
XLA Ops:
  6.5 0.0 copy-start
  6.5 0.0 reduce-scatter.2.cloned.1.call-start
  6.5 1.2 fusion.4
  7.8 1.2 fusion.5
  9.0 1.1 fusion.6
  10.1 1.2 fusion.7
  11.3 1.2 constant_dynamic-update-slice_fusion
  12.5 0.0 copy-done
  12.5 0.1 fusion.8
  12.6 0.1 fusion.9
  12.7 0.1 fusion.10
  12.7 0.1 fusion.11
  12.8 7.4 %copy.9 = f32[8,7,7,4608]{3,2,1,0:T(8,128)} copy(f32[8,7,7,4608]{3,0,2,1:T(8,128)S(1)} %fusion.11) | data formatting | bytes 14450688 | tf_op jit(solution)/shard_map/concatenate | solution.py:17
  20.3 0.0 copy-start.1
  20.3 9.1 %reshape.158 = f32[392,4608]{1,0:T(8,128)} reshape(f32[8,7,7,4608]{3,2,1,0:T(8,128)} %copy.9) | data formatting | bytes 14450688 | tf_op jit(solution)/shard_map/reshape | solution.py:17
  29.4 0.0 copy-done.1
  29.4 1.4 copy.10
  30.8 0.0 slice-start
  30.8 2.3 reshape.160
  33.1 0.0 slice-start.1
  33.1 12.5 %convolution_subtract_fusion = f32[392,512]{1,0:T(8,128)S(1)} fusion(f32[392,512]{1,0:T(8,128)} %reshape.160, f32[392,4608]{1,0:T(8,128)} %reshape.158, f32[4608,512]{1,0:T(8,128)} %bitcast.44), kind=kOutput, calls=%fused_computation.9 | convolution fusion | flops 5549264896 | bytes 18268160 | tf_op jit(solution)/shard_map/dot_general | solution.py:38
  45.6 0.0 slice-done
  45.6 0.0 slice-done.1
  45.6 10.3 %convolution_multiply_fusion = f32[4608,512]{1,0:T(8,128)} fusion(f32[392,4608]{1,0:T(8,128)S(1)} %bitcast.43, f32[392,512]{1,0:T(8,128)S(1)} %convolution_subtract_fusion), kind=kOutput, calls=%fused_computation | convolution fusion | flops 5551423488 | bytes 17465344 | tf_op jit(solution)/shard_map/dot_general | solution.py:40
  55.9 0.0 reduce-scatter.2.cloned.1.call-update
  55.9 107.0 %reduce-scatter.2.cloned.1.call-done = f32[288,512]{1,0:T(8,128)} async-done(((f32[4608,512]{1,0:T(8,128)}), f32[288,512]{1,0:T(8,128)}) %reduce-scatter.2.cloned.1.call-update) | async-done | bytes 589840 | tf_op jit(solution)/shard_map/reduce_scatter | solution.py:43
  162.9 2.2 copy.11
  165.2 14.2 %all-to-all-start = ((f32[32,288,16]{1,2,0:T(8,128)}), f32[32,288,16]{1,2,0:T(8,128)S(1)}, u32[]{:S(2)}, u32[]{:S(2)}) async-start(f32[32,288,16]{1,2,0:T(8,128)} %bitcast.2), calls=%async_computation.1 | async-start | bytes 1572864 | tf_op jit(solution)/shard_map/all_to_all | solution.py:45
  179.4 44.5 %all-to-all-done = f32[32,288,16]{1,2,0:T(8,128)S(1)} async-done(((f32[32,288,16]{1,2,0:T(8,128)}), f32[32,288,16]{1,2,0:T(8,128)S(1)}, u32[]{:S(2)}, u32[]{:S(2)}) %all-to-all-start) | async-done | bytes 589856 | tf_op jit(solution)/shard_map/all_to_all | solution.py:45
  224.0 0.9 convolution_bitcast_fusion
  224.9 99.5 %psum.7 = f32[32,32]{1,0:T(8,128)S(1)} all-reduce(f32[32,32]{1,0:T(8,128)S(1)} %convolution_bitcast_fusion), channel_id=1, replica_groups=mesh['node'=32,'local'=16] {'node','local'}, use_global_device_ids=true, to_apply=%region_1.2 | all-reduce | flops 1024 | bytes 8192 | tf_op jit(solution)/shard_map/psum | solution.py:47
  324.4 0.2 fusion
  324.7 0.2 multiply_reduce_fusion.1
  324.9 0.1 multiply_add_fusion
  325.1 0.2 fusion.1
  325.3 0.3 multiply_reduce_fusion.3
  325.6 0.1 multiply_add_fusion.1
  325.7 0.2 fusion.2
  326.0 0.3 multiply_reduce_fusion.5
  326.3 0.1 multiply_add_fusion.2
  326.4 0.2 fusion.3
  326.7 0.3 multiply_reduce_fusion.7
  327.0 0.1 multiply_add_fusion.3
  327.0 0.8 multiply_reduce_fusion.9
  327.9 0.7 fusion.13
  331.2 0.7 multiply_reduce_fusion
  (18 shorter events, 0.3 us)
Async XLA Ops:
  6.5 6.0 %copy-start = (f32[8,7,7,512]{3,0,2,1:T(8,128)S(1)}, f32[8,7,7,512]{3,0,2,1:T(8,128)}, u32[]{:S(2)}) copy-start(f32[8,7,7,512]{3,0,2,1:T(8,128)} %param.3) | copy-start | bytes 2408452
  6.5 156.4 %reduce-scatter.2.cloned.1.call-start = ((), (), s32[]{:S(2)}) async-start(), calls=%async_computation.2 | async-start | bytes 10027008 | tf_op jit(solution)/shard_map/reduce_scatter | solution.py:43
  20.3 9.1 %copy-start.1 = (f32[8,7,7,512]{3,0,2,1:T(8,128)S(1)}, f32[8,7,7,512]{3,0,2,1:T(8,128)}, u32[]{:S(2)}) copy-start(f32[8,7,7,512]{3,0,2,1:T(8,128)} %param.4) | copy-start | bytes 2408452
  30.8 14.8 %slice-start = ((s8[7225344]{0:T(1024)(128)(4,1)}), s8[3031040]{0:T(1024)(128)(4,1)S(1)}, s32[]{:S(2)}) async-start(s8[7225344]{0:T(1024)(128)(4,1)} %bitcast.42), calls=%async_computation.3 | async-start | bytes 6062080
  33.1 12.5 %slice-start.1 = ((s8[7225344]{0:T(1024)(128)(4,1)}), s8[4194304]{0:T(1024)(128)(4,1)S(1)}, s32[]{:S(2)}) async-start(s8[7225344]{0:T(1024)(128)(4,1)} %bitcast.42), calls=%async_computation.4 | async-start | bytes 8388608
  165.2 58.8 %all-to-all-start = ((f32[32,288,16]{1,2,0:T(8,128)}), f32[32,288,16]{1,2,0:T(8,128)S(1)}, u32[]{:S(2)}, u32[]{:S(2)}) async-start(f32[32,288,16]{1,2,0:T(8,128)} %bitcast.2), calls=%async_computation.1 | async-start | bytes 1572864 | tf_op jit(solution)/shard_map/all_to_all | solution.py:45
Sparse Core Ops, SparseCore 0:
  56.1 106.8 reduce-scatter.1

commit v2 on v1

v2 whole, which is shorter than its diff:
```python
import jax
import jax.numpy as jnp
from jax import lax
from jax.experimental import pallas as pl
from jax.experimental.pallas import tpu as pltpu
from jax.sharding import PartitionSpec as P

F32, BF16 = jnp.float32, jnp.bfloat16
EPS = 1e-06
SIDE, IMG, C, TAPS = 7, 8, 512, 9
N_NODE, N_LOCAL, RING = 32, 16, 4
ROWS_L = TAPS * C // N_LOCAL
HALF = C // 2
GRID = 8 * IMG
PAD_ROWS = 10 * GRID + 2 * IMG
OUT_ROWS = SIDE * GRID
CHUNKS = ((256, 32), (0, 64), (64, 64), (128, 64), (192, 64))
NQ = len(CHUNKS)
BASE = (0, 32, 96, 160, 224)
MESH = pl.DeviceIdType.MESH


def split(value):
    hi = value.astype(BF16)
    return hi, (value - hi.astype(F32)).astype(BF16)


def dot(a, b):
    return jnp.dot(a, b, preferred_element_type=F32)


def kernel(
    x_hbm, t_hbm, w_hbm, out_ref,
    xin, tin, wbuf, xs_hi, xs_lo, xt_hi, xt_lo, acc, r_hi, r_lo, g, p1, p2, zs, zr, gram, sb, s1, s2, s3,
    in_sem, p1_send, p1_recv, p2_send, p2_recv, z_send, z_recv, s_send, s_recv,
):
    node, local = lax.axis_index("node"), lax.axis_index("local")
    y, x = local // RING, lax.rem(local, RING)

    def at(yy, xx):
        return lax.rem(yy + RING, RING) * RING + lax.rem(xx + RING, RING)

    neighbours = ((at(y, x + 1), at(y, x - 1)), (at(y + 1, x), at(y - 1, x)))

    x_copy = pltpu.make_async_copy(x_hbm, xin, in_sem.at[0])
    t_copy = pltpu.make_async_copy(t_hbm, tin, in_sem.at[1])
    x_copy.start()
    for t in range(TAPS):
        pltpu.make_async_copy(w_hbm.at[t], wbuf.at[t], in_sem.at[2 + t]).start()
    t_copy.start()

    barrier = pltpu.get_barrier_semaphore()

    @pl.loop(1, N_LOCAL)
    def _(d):
        pl.semaphore_signal(barrier, inc=1, device_id={"local": lax.rem(local + d, N_LOCAL)}, device_id_type=MESH)

    @pl.loop(1, N_NODE)
    def _(d):
        pl.semaphore_signal(barrier, inc=1, device_id={"node": lax.rem(node + d, N_NODE)}, device_id_type=MESH)

    zero = jnp.zeros((2 * GRID, C), BF16)
    for ref in (xs_hi, xs_lo):
        for first in (0, PAD_ROWS):
            ref[first : first + GRID, :] = zero[:GRID]
            ref[first + 8 * GRID : first + 10 * GRID, :] = zero
            ref[first + 10 * GRID : first + PAD_ROWS, :] = zero[: 2 * IMG]
    r_hi[OUT_ROWS:, :] = zero[:GRID]
    r_lo[OUT_ROWS:, :] = zero[:GRID]
    acc[...] = jnp.zeros_like(acc)
    gram[...] = jnp.zeros_like(gram)
    x_copy.wait()
    edge = jnp.zeros((IMG, C), F32)

    @pl.loop(0, SIDE)
    def _(r):
        row = xin[r].reshape(SIDE * IMG, C)
        even = split(jnp.concatenate([edge, row], axis=0))
        odd = split(jnp.concatenate([row, edge], axis=0))
        first = pl.multiple_of((r + 1) * GRID, GRID)
        for ref, e, o in ((xs_hi, even[0], odd[0]), (xs_lo, even[1], odd[1])):
            ref[pl.ds(first, GRID), :] = e
            ref[pl.ds(pl.multiple_of(PAD_ROWS + first, 2 * IMG), GRID), :] = o

    @pl.loop(0, TAPS)
    def _(t):
        i, j = t // 3, lax.rem(t, 3)
        start = i * GRID + jnp.where(j == 1, PAD_ROWS, j * IMG)
        start = pl.multiple_of(start, 2 * IMG)
        pltpu.make_async_copy(w_hbm.at[t], wbuf.at[t], in_sem.at[2 + t]).wait()
        w_hi, w_lo = split(wbuf[t])
        x_hi = xs_hi[pl.ds(start, OUT_ROWS), :]
        x_lo = xs_lo[pl.ds(start, OUT_ROWS), :]
        acc[...] += dot(x_hi, w_hi) + dot(x_hi, w_lo) + dot(x_lo, w_hi)
        rows = pl.ds(pl.multiple_of(t * C, C), C)
        xt_hi[rows, :] = xs_hi[pl.ds(start, C), :].T
        xt_lo[rows, :] = xs_lo[pl.ds(start, C), :].T

    t_copy.wait()
    source = lax.broadcasted_iota(jnp.int32, (C, C), 0)
    place = lax.broadcasted_iota(jnp.int32, (C, C), 1)
    wanted = ((place & (HALF - 1)) >> 3) * 16 + (place >> 8) * 8 + (place & 7)
    order = jnp.where(source == wanted, 1.0, 0.0).astype(BF16)
    scale = 1.0 / (SIDE * SIDE * IMG)

    for r in range(SIDE):
        diff = (acc[r * GRID : r * GRID + SIDE * IMG, :] - tin[r].reshape(SIDE * IMG, C)) * scale
        hi, lo = split(jnp.concatenate([diff, edge], axis=0))
        r_hi[r * GRID : (r + 1) * GRID, :] = hi
        r_lo[r * GRID : (r + 1) * GRID, :] = lo
    r_hi[:OUT_ROWS, :] = dot(r_hi[:OUT_ROWS, :], order).astype(BF16)
    r_lo[:OUT_ROWS, :] = dot(r_lo[:OUT_ROWS, :], order).astype(BF16)

    pl.semaphore_wait(barrier, N_LOCAL + N_NODE - 2)

    def block(q, h, i, j0, j1):
        m = CHUNKS[q][1]
        first = 16 * BASE[q] + (4 * i + j0) * m
        return g.at[h, first : first + (j1 - j0) * m, :]

    def kept(q, h, j, u):
        m = CHUNKS[q][1]
        first = 16 * BASE[q] + j * m + u * (m // 2)
        return g.at[h, first : first + m // 2, :]

    def p1_slot(q, h, kind):
        m = CHUNKS[q][1]
        first = 12 * BASE[q] + kind * 2 * m
        return p1.at[h, first : first + 2 * m, :]

    def p2_slot(q, h, kind):
        m = CHUNKS[q][1]
        first = 3 * BASE[q] + kind * (m // 2)
        return p2.at[h, first : first + m // 2, :]

    P1_PART = ((2, 0, 2), (2, 2, 4), (1, 2, 4), (3, 0, 2), (1, 0, 2), (3, 2, 4))
    P2_PART = ((2, 0), (2, 1), (1, 1), (3, 0), (1, 0), (3, 1))

    def p1_copy(q, h, kind):
        n = (q * 2 + h) * 6 + kind
        return pltpu.make_async_remote_copy(
            src_ref=block(q, h, *P1_PART[kind]), dst_ref=p1_slot(q, h, kind),
            send_sem=p1_send.at[n], recv_sem=p1_recv.at[n],
            device_id={"local": neighbours[h][kind % 2]}, device_id_type=MESH,
        )

    def p2_copy(q, h, kind):
        n = (q * 2 + h) * 6 + kind
        return pltpu.make_async_remote_copy(
            src_ref=kept(q, h, *P2_PART[kind]), dst_ref=p2_slot(q, h, kind),
            send_sem=p2_send.at[n], recv_sem=p2_recv.at[n],
            device_id={"local": neighbours[1 - h][kind % 2]}, device_id_type=MESH,
        )

    def gradient(q, h, i):
        first, m = CHUNKS[q]
        parts_hi, parts_lo = [], []
        for j in range(RING):
            owner = at(y + j, x + i) if h == 0 else at(y + i, x + j)
            rows = pl.ds(pl.multiple_of(owner * ROWS_L + first, 32), m)
            parts_hi.append(xt_hi[rows, :])
            parts_lo.append(xt_lo[rows, :])
        a_hi = jnp.concatenate(parts_hi, axis=0)
        a_lo = jnp.concatenate(parts_lo, axis=0)
        cols = slice(h * HALF, (h + 1) * HALF)
        b_hi, b_lo = r_hi[:, cols], r_lo[:, cols]
        block(q, h, i, 0, 4)[...] = dot(a_hi, b_hi) + dot(a_hi, b_lo) + dot(a_lo, b_hi)

    def stage1(q):
        for h in range(2):
            gradient(q, h, 2)
            p1_copy(q, h, 0).start()
            p1_copy(q, h, 1).start()
        for h in range(2):
            gradient(q, h, 1)
            p1_copy(q, h, 2).start()
            gradient(q, h, 3)
            p1_copy(q, h, 3).start()
        for h in range(2):
            gradient(q, h, 0)

    def stage2(q):
        for h in range(2):
            for side in range(2):
                p1_copy(q, h, side).wait_recv()
                block(q, h, *P1_PART[4 + side])[...] += p1_slot(q, h, side)[...]
                p1_copy(q, h, 4 + side).start()

    def stage3(q):
        for h in range(2):
            for kind in (2, 3, 4, 5):
                p1_copy(q, h, kind).wait_recv()
            block(q, h, 0, 2, 4)[...] += p1_slot(q, h, 2)[...] + p1_slot(q, h, 5)[...]
            p2_copy(q, h, 0).start()
            p2_copy(q, h, 1).start()
            block(q, h, 0, 0, 2)[...] += p1_slot(q, h, 3)[...] + p1_slot(q, h, 4)[...]
            p2_copy(q, h, 2).start()
            p2_copy(q, h, 3).start()

    def stage4(q):
        for h in range(2):
            for side in range(2):
                p2_copy(q, h, side).wait_recv()
                kept(q, h, *P2_PART[4 + side])[...] += p2_slot(q, h, side)[...]
                p2_copy(q, h, 4 + side).start()

    def z_copy(q, peer):
        return pltpu.make_async_remote_copy(
            src_ref=zs.at[q, pl.ds(pl.multiple_of(peer * 8, 8), 8), :], dst_ref=zr.at[q, node],
            send_sem=z_send.at[q], recv_sem=z_recv.at[q],
            device_id={"node": peer}, device_id_type=MESH,
        )

    def stage5(q):
        m = CHUNKS[q][1]
        parts = []
        for h in range(2):
            for kind in (2, 3, 4, 5):
                p2_copy(q, h, kind).wait_recv()
            parts.append(kept(q, h, 0, 0)[...] + p2_slot(q, h, 3)[...] + p2_slot(q, h, 4)[...])
            parts.append(kept(q, h, 0, 1)[...] + p2_slot(q, h, 2)[...] + p2_slot(q, h, 5)[...])
            if m < 64:
                parts.append(jnp.zeros((64 - m, HALF), F32))
        zs[q] = jnp.concatenate(parts, axis=0).T

        @pl.loop(1, N_NODE)
        def _(d):
            z_copy(q, lax.rem(node + d, N_NODE)).start()

        zr[q, node] = zs[q, pl.ds(pl.multiple_of(node * 8, 8), 8), :]

    def wait_blocks(ref, count, sem):
        part = ref.at[pl.ds(0, count)]
        pltpu.make_async_copy(part, part, sem).wait()

    def stage6(q):
        wait_blocks(zr.at[q], N_NODE - 1, z_recv.at[q])
        wide = jnp.concatenate([zr[q, :, s, :] for s in range(8)], axis=1)
        gram[:, :N_NODE] += lax.dot_general(
            wide, wide, (((1,), (1,)), ((), ())), precision=lax.Precision.HIGHEST, preferred_element_type=F32
        )

    for step in range(NQ + 4):
        if step < NQ:
            stage1(step)
            stage2(step)
        if 0 <= step - 2 < NQ:
            stage4(step - 2)
        if 0 <= step - 1 < NQ:
            stage3(step - 1)
        if 0 <= step - 3 < NQ:
            stage5(step - 3)
        if 0 <= step - 4 < NQ:
            stage6(step - 4)

    def exchange(n, value, buf, count, slot, peer):
        sb[n] = value
        buf[slot] = value

        @pl.loop(1, count)
        def _(d):
            pltpu.make_async_remote_copy(
                src_ref=sb.at[n], dst_ref=buf.at[slot], send_sem=s_send.at[n], recv_sem=s_recv.at[n],
                device_id=peer(d), device_id_type=MESH,
            ).start()

        wait_blocks(buf, count - 1, s_recv.at[n])
        total = buf[0]
        for k in range(1, count):
            total = total + buf[k]
        return total

    packed = gram[0:8, :]
    for k in range(1, 4):
        packed = packed + pltpu.roll(gram[8 * k : 8 * k + 8, :], 32 * k, 1)
    group, member = node // 8, lax.rem(node, 8)
    packed = exchange(0, packed, s1, 8, member, lambda d: {"node": group * 8 + lax.rem(member + d, 8)})
    packed = exchange(1, packed, s2, 4, group, lambda d: {"node": lax.rem(group + d, 4) * 8 + member})
    packed = exchange(2, packed, s3, N_LOCAL, local, lambda d: {"local": lax.rem(local + d, N_LOCAL)})

    lane8 = lax.broadcasted_iota(jnp.int32, (8, 128), 1)
    pieces = []
    for k in range(4):
        turned = packed if k == 0 else pltpu.roll(packed, 128 - 32 * k, 1)
        pieces.append(jnp.where(lane8 < N_NODE, turned, 0.0))
    products = jnp.concatenate(pieces, axis=0)
    row = lax.broadcasted_iota(jnp.int32, (N_NODE, 128), 0)
    col = lax.broadcasted_iota(jnp.int32, (N_NODE, 128), 1)
    coefs = jnp.ones((N_NODE, 1), F32)
    level = 1
    while level < N_NODE:
        own = jnp.where(row == col, products, 0.0)
        cross = jnp.where(col == (row ^ level), products, 0.0)

        def weight(axis):
            square = jnp.maximum(jnp.sum(own, axis=axis, keepdims=True), 0.0)
            return 1.0 - jnp.sum(cross, axis=axis, keepdims=True) / (2.0 * (square + EPS))

        down = weight(1)
        coefs = coefs * down
        products = products * down * weight(0)
        products = products + jnp.where(
            (col & level) != 0, pltpu.roll(products, level, 1), pltpu.roll(products, 128 - level, 1)
        )
        products = products + jnp.where(
            (row & level) != 0, pltpu.roll(products, level, 0), pltpu.roll(products, N_NODE - level, 0)
        )
        level *= 2

    spread = jnp.broadcast_to(coefs, (N_NODE, 128))
    merged = []
    for q in range(NQ):
        total = spread[0:1, :] * zr[q, 0]
        for n in range(1, N_NODE):
            total = total + spread[n : n + 1, :] * zr[q, n]
        merged.append(total)
    for a in range(2):
        for q in range(NQ):
            first, m = CHUNKS[q]
            out_ref[8 * a : 8 * a + 8, first : first + m] = merged[q][:, 64 * a : 64 * a + m]

    for q in range(NQ):
        for h in range(2):
            for kind in range(6):
                p1_copy(q, h, kind).wait_send()
                p2_copy(q, h, kind).wait_send()
        wait_blocks(zr.at[q], N_NODE - 1, z_send.at[q])
    for n, (buf, count) in enumerate(((s1, 8), (s2, 4), (s3, N_LOCAL))):
        wait_blocks(buf, count - 1, s_send.at[n])


def on_device(images, targets, weight):
    any_spec = pl.BlockSpec(memory_space=pl.ANY)
    dma = pltpu.SemaphoreType.DMA
    vmem = pltpu.VMEM
    out = pl.pallas_call(
        kernel,
        out_shape=jax.ShapeDtypeStruct((C // N_NODE, ROWS_L), F32),
        in_specs=[any_spec] * 3,
        out_specs=pl.BlockSpec(memory_space=pltpu.VMEM),
        scratch_shapes=[
            vmem((SIDE, SIDE, IMG, C), F32), vmem((SIDE, SIDE, IMG, C), F32), vmem((TAPS, C, C), F32),
            vmem((2 * PAD_ROWS, C), BF16), vmem((2 * PAD_ROWS, C), BF16),
            vmem((TAPS * C, C), BF16), vmem((TAPS * C, C), BF16),
            vmem((OUT_ROWS, C), F32), vmem((C, C), BF16), vmem((C, C), BF16),
            vmem((2, 16 * ROWS_L, HALF), F32), vmem((2, 12 * ROWS_L, HALF), F32), vmem((2, 3 * ROWS_L, HALF), F32),
            vmem((NQ, HALF, 128), F32), vmem((NQ, N_NODE, 8, 128), F32),
            vmem((N_NODE, 128), F32), vmem((3, 8, 128), F32),
            vmem((8, 8, 128), F32), vmem((4, 8, 128), F32), vmem((N_LOCAL, 8, 128), F32),
            dma((2 + TAPS,)), dma((12 * NQ,)), dma((12 * NQ,)), dma((12 * NQ,)), dma((12 * NQ,)),
            dma((NQ,)), dma((NQ,)), dma((3,)), dma((3,)),
        ],
        compiler_params=pltpu.CompilerParams(collective_id=0, has_side_effects=True, vmem_limit_bytes=56 * 2**20),
        cost_estimate=pl.CostEstimate(flops=12 * 10**9, bytes_accessed=12 * 10**6, transcendentals=0),
    )(
        jnp.transpose(images, (1, 2, 0, 3)),
        jnp.transpose(targets, (1, 2, 0, 3)),
        weight.reshape(TAPS, C, C),
    )
    return out.T


def solution(mesh):
    image_spec = P(("node", "local"), None, None, None)
    return jax.shard_map(
        on_device, mesh=mesh, in_specs=(image_spec, image_spec, P()), out_specs=P("local", "node"), check_vma=False
    )
```

time: 339 us -> 115 us (0.34)
  waiting for transfers between devices: 152 us -> 0 us
  Pallas kernels: 0 us -> 113 us
  blocking collectives: 99.5 us -> 0 us
  local copies, waits for them, and re-layouts: 28.9 us -> 1.35 us
  matrix products: 27.3 us -> 0 us
  between operations: 16.2 us -> 0.01 us
  starting transfers between devices: 14.2 us -> 0 us
    pallas_call x0 -> x1, Pallas kernels: none -> 113 us  [on_device(): pl.pallas_call(kernel, out_shape=jax.ShapeDtypeStruct((C // N_NODE, ROWS_...]
    reduce_scatter x1 -> x0, waiting for transfers between devices: 107 us -> none  [on_device(): lax.psum_scatter(product * (1.0 / patches.shape[0]), 'local', scatter_dim...]
    psum x1 -> x0, blocking collectives: 99.5 us -> none  [on_device(): lax.psum(lax.dot_general(flat, flat, (((1,), (1,)), ((), ())), precision=...]
    all_to_all x1 -> x0, waiting for transfers between devices: 44.5 us -> none  [on_device(): blocks = lax.all_to_all(split, 'node', 0, 0, tiled=True)]
    dot_general x13 -> x0, matrix products: 27.3 us -> none  [the longest x1 12.5 us: on_device(): jnp.dot(patches, flat_w, precision=lax.Precision.HIGH, preferred_element_...]
    all_to_all x1 -> x0, starting transfers between devices: 14.2 us -> none  [on_device(): blocks = lax.all_to_all(split, 'node', 0, 0, tiled=True)]
    reshape x2 -> x0, local copies, waits for them, and re-layouts: 11.5 us -> none  [the longest x1 9.12 us: make_patches(): return jnp.concatenate(views, axis=-1).reshape(-1, 9 * images.shape[3])]
    concatenate x2 -> x0, local copies, waits for them, and re-layouts: 7.5 us -> none  [make_patches(): return jnp.concatenate(views, axis=-1).reshape(-1, 9 * images.shape[3])]
  transfers between devices with their start and end apart: 2 -> 0, of which waited for: 2 -> 0; matrix products, arithmetic and copies ran while one was open for 0% -> 0% of each run, Pallas kernels for 0% -> 0%
where the time goes in v2:
time: 115 us; the launch traced here: 114 us
  Pallas kernels  113 us (98%)
  local copies, waits for them, and re-layouts  1.35 us (1%)
    pallas_call x1, Pallas kernels, on_device(): pl.pallas_call(kernel, out_shape=jax.ShapeDtypeStruct((C // N_NODE, ROWS_...  113 us

profile of v2, /device:TPU:1, one launch (start us, length us, event | category | flops | bytes accessed | tf_op | source)
XLA Modules:
  0.0 113.9 jit_solution(4341717855309664064)
XLA Ops:
  0.0 112.6 %shard_map.37 = f32[16,288]{1,0:T(8,128)} custom-call(f32[7,7,8,512]{3,2,1,0:T(8,128)} %bitcast.6, f32[7,7,8,512]{3,2,1,0:T(8,128)} %bitcast.7, f32[9,512,512]{2,1,0:T(8,128)} %bitcast.5), custom_call_target="tpu_custom_call" | custom-call | flops 12000000000 | bytes 12000000 | tf_op jit(solution)/shard_map/pallas_call | solution.py:336
  112.6 1.3 %copy.5 = f32[288,16]{0,1:T(8,128)} copy(f32[288,16]{0,1:T(8,128)} %bitcast.4) | data formatting | bytes 36864

commit v3 on v2

--- a/solution.py
+++ b/solution.py
@@ -14,9 +14,11 @@
 GRID = 8 * IMG
 PAD_ROWS = 10 * GRID + 2 * IMG
 OUT_ROWS = SIDE * GRID
-CHUNKS = ((256, 32), (0, 64), (64, 64), (128, 64), (192, 64))
+CHUNKS = ((0, 64), (64, 64), (128, 64), (192, 64), (256, 32))
 NQ = len(CHUNKS)
-BASE = (0, 32, 96, 160, 224)
+LAST = NQ - 1
+P2_KINDS = (6, 6, 6, 6, 3)
+BASE = (0, 64, 128, 192, 256)
 MESH = pl.DeviceIdType.MESH
 
 
@@ -31,7 +33,7 @@
 
 def kernel(
     x_hbm, t_hbm, w_hbm, out_ref,
-    xin, tin, wbuf, xs_hi, xs_lo, xt_hi, xt_lo, acc, r_hi, r_lo, g, p1, p2, zs, zr, gram, sb, s1, s2, s3,
+    xin, tin, wbuf, xs_hi, xs_lo, xt_hi, xt_lo, acc, r_hi, r_lo, g, p1, p2, zs, zr, zs_last, zr_last, gram, sb, s1, s2, s3,
     in_sem, p1_send, p1_recv, p2_send, p2_recv, z_send, z_recv, s_send, s_recv,
 ):
     node, local = lax.axis_index("node"), lax.axis_index("local")
@@ -40,7 +42,7 @@
     def at(yy, xx):
         return lax.rem(yy + RING, RING) * RING + lax.rem(xx + RING, RING)
 
-    neighbours = ((at(y, x + 1), at(y, x - 1)), (at(y + 1, x), at(y - 1, x)))
+    neighbours = ((at(y, x + 1), at(y, x - 1), at(y, x + 2)), (at(y + 1, x), at(y - 1, x), at(y + 2, x)))
 
     x_copy = pltpu.make_async_copy(x_hbm, xin, in_sem.at[0])
     t_copy = pltpu.make_async_copy(t_hbm, tin, in_sem.at[1])
@@ -82,19 +84,21 @@
             ref[pl.ds(first, GRID), :] = e
             ref[pl.ds(pl.multiple_of(PAD_ROWS + first, 2 * IMG), GRID), :] = o
 
-    @pl.loop(0, TAPS)
-    def _(t):
-        i, j = t // 3, lax.rem(t, 3)
-        start = i * GRID + jnp.where(j == 1, PAD_ROWS, j * IMG)
-        start = pl.multiple_of(start, 2 * IMG)
-        pltpu.make_async_copy(w_hbm.at[t], wbuf.at[t], in_sem.at[2 + t]).wait()
-        w_hi, w_lo = split(wbuf[t])
-        x_hi = xs_hi[pl.ds(start, OUT_ROWS), :]
-        x_lo = xs_lo[pl.ds(start, OUT_ROWS), :]
-        acc[...] += dot(x_hi, w_hi) + dot(x_hi, w_lo) + dot(x_lo, w_hi)
-        rows = pl.ds(pl.multiple_of(t * C, C), C)
-        xt_hi[rows, :] = xs_hi[pl.ds(start, C), :].T
-        xt_lo[rows, :] = xs_lo[pl.ds(start, C), :].T
+    @pl.loop(0, 3)
+    def _(i):
+        total = acc[...]
+        for j in range(3):
+            t = 3 * i + j
+            start = pl.multiple_of(i * GRID + (PAD_ROWS if j == 1 else j * IMG), 2 * IMG)
+            pltpu.make_async_copy(w_hbm.at[t], wbuf.at[t], in_sem.at[2 + t]).wait()
+            w_hi, w_lo = split(wbuf[t])
+            x_hi = xs_hi[pl.ds(start, OUT_ROWS), :]
+            x_lo = xs_lo[pl.ds(start, OUT_ROWS), :]
+            total = total + (dot(x_hi, w_hi) + dot(x_hi, w_lo) + dot(x_lo, w_hi))
+            rows = pl.ds(pl.multiple_of(t * C, C), C)
+            xt_hi[rows, :] = xs_hi[pl.ds(start, C), :].T
+            xt_lo[rows, :] = xs_lo[pl.ds(start, C), :].T
+        acc[...] = total
 
     t_copy.wait()
     source = lax.broadcasted_iota(jnp.int32, (C, C), 0)
@@ -111,8 +115,6 @@
     r_hi[:OUT_ROWS, :] = dot(r_hi[:OUT_ROWS, :], order).astype(BF16)
     r_lo[:OUT_ROWS, :] = dot(r_lo[:OUT_ROWS, :], order).astype(BF16)
 
-    pl.semaphore_wait(barrier, N_LOCAL + N_NODE - 2)
-
     def block(q, h, i, j0, j1):
         m = CHUNKS[q][1]
         first = 16 * BASE[q] + (4 * i + j0) * m
@@ -130,6 +132,8 @@
 
     def p2_slot(q, h, kind):
         m = CHUNKS[q][1]
+        if q == LAST:
+            return p2.at[h, 3 * BASE[q] + kind * m : 3 * BASE[q] + (kind + 1) * m, :]
         first = 3 * BASE[q] + kind * (m // 2)
         return p2.at[h, first : first + m // 2, :]
 
@@ -146,10 +150,14 @@
 
     def p2_copy(q, h, kind):
         n = (q * 2 + h) * 6 + kind
+        if q == LAST:
+            src, hop = block(q, h, 0, (1, 3, 2)[kind], (1, 3, 2)[kind] + 1), kind
+        else:
+            src, hop = kept(q, h, *P2_PART[kind]), kind % 2
         return pltpu.make_async_remote_copy(
-            src_ref=kept(q, h, *P2_PART[kind]), dst_ref=p2_slot(q, h, kind),
+            src_ref=src, dst_ref=p2_slot(q, h, kind),
             send_sem=p2_send.at[n], recv_sem=p2_recv.at[n],
-            device_id={"local": neighbours[1 - h][kind % 2]}, device_id_type=MESH,
+            device_id={"local": neighbours[1 - h][hop]}, device_id_type=MESH,
         )
 
     def gradient(q, h, i):
@@ -169,15 +177,20 @@
     def stage1(q):
         for h in range(2):
             gradient(q, h, 2)
+            if q == h == 0:
+                pl.semaphore_wait(barrier, N_LOCAL + N_NODE - 2)
             p1_copy(q, h, 0).start()
             p1_copy(q, h, 1).start()
-        for h in range(2):
-            gradient(q, h, 1)
+
+    def stage1_rest(q):
+        for h in range(2):
+            for i in (1, 3, 0):
+                gradient(q, h, i)
+
+    def stage1_send(q):
+        for h in range(2):
             p1_copy(q, h, 2).start()
-            gradient(q, h, 3)
             p1_copy(q, h, 3).start()
-        for h in range(2):
-            gradient(q, h, 0)
 
     def stage2(q):
         for h in range(2):
@@ -191,6 +204,11 @@
             for kind in (2, 3, 4, 5):
                 p1_copy(q, h, kind).wait_recv()
             block(q, h, 0, 2, 4)[...] += p1_slot(q, h, 2)[...] + p1_slot(q, h, 5)[...]
+            if q == LAST:
+                block(q, h, 0, 0, 2)[...] += p1_slot(q, h, 3)[...] + p1_slot(q, h, 4)[...]
+                for kind in (2, 0, 1):
+                    p2_copy(q, h, kind).start()
+                continue
             p2_copy(q, h, 0).start()
             p2_copy(q, h, 1).start()
             block(q, h, 0, 0, 2)[...] += p1_slot(q, h, 3)[...] + p1_slot(q, h, 4)[...]
@@ -198,6 +216,8 @@
             p2_copy(q, h, 3).start()
 
     def stage4(q):
+        if q == LAST:
+            return
         for h in range(2):
             for side in range(2):
                 p2_copy(q, h, side).wait_recv()
@@ -205,9 +225,12 @@
                 p2_copy(q, h, 4 + side).start()
 
     def z_copy(q, peer):
+        if q == LAST:
+            src, dst = zs_last.at[peer], zr_last.at[node]
+        else:
+            src, dst = zs.at[q, pl.ds(pl.multiple_of(peer * 8, 8), 8), :], zr.at[q, node]
         return pltpu.make_async_remote_copy(
-            src_ref=zs.at[q, pl.ds(pl.multiple_of(peer * 8, 8), 8), :], dst_ref=zr.at[q, node],
-            send_sem=z_send.at[q], recv_sem=z_recv.at[q],
+            src_ref=src, dst_ref=dst, send_sem=z_send.at[q], recv_sem=z_recv.at[q],
             device_id={"node": peer}, device_id_type=MESH,
         )
 
@@ -215,43 +238,65 @@
         m = CHUNKS[q][1]
         parts = []
         for h in range(2):
+            if q == LAST:
+                for kind in (0, 1, 2):
+                    p2_copy(q, h, kind).wait_recv()
+                parts.append(
+                    block(q, h, 0, 0, 1)[...] + p2_slot(q, h, 0)[...] + p2_slot(q, h, 1)[...] + p2_slot(q, h, 2)[...]
+                )
+                continue
             for kind in (2, 3, 4, 5):
                 p2_copy(q, h, kind).wait_recv()
             parts.append(kept(q, h, 0, 0)[...] + p2_slot(q, h, 3)[...] + p2_slot(q, h, 4)[...])
             parts.append(kept(q, h, 0, 1)[...] + p2_slot(q, h, 2)[...] + p2_slot(q, h, 5)[...])
-            if m < 64:
-                parts.append(jnp.zeros((64 - m, HALF), F32))
-        zs[q] = jnp.concatenate(parts, axis=0).T
-
-        @pl.loop(1, N_NODE)
-        def _(d):
-            z_copy(q, lax.rem(node + d, N_NODE)).start()
-
-        zr[q, node] = zs[q, pl.ds(pl.multiple_of(node * 8, 8), 8), :]
+        if q == LAST:
+            parts.append(jnp.zeros((64, HALF), F32))
+            turned = jnp.concatenate(parts, axis=0).T
+            behind = pltpu.roll(turned, 64, 1)
+            zs_last[...] = turned.reshape(N_NODE, 8, 128)[:, 0:4, :] + behind.reshape(N_NODE, 8, 128)[:, 4:8, :]
+        else:
+            zs[q] = jnp.concatenate(parts, axis=0).T
+
+        @pl.loop(0, N_NODE - 1)
+        def _(k):
+            far = N_NODE // 2 + jnp.where(lax.rem(k, 2) == 1, (k + 1) // 2, -((k + 1) // 2))
+            z_copy(q, lax.rem(node + far, N_NODE)).start()
+
+        if q == LAST:
+            zr_last[node] = zs_last[node]
+        else:
+            zr[q, node] = zs[q, pl.ds(pl.multiple_of(node * 8, 8), 8), :]
 
     def wait_blocks(ref, count, sem):
         part = ref.at[pl.ds(0, count)]
         pltpu.make_async_copy(part, part, sem).wait()
 
+    def landed(q):
+        return zr_last if q == LAST else zr.at[q]
+
     def stage6(q):
-        wait_blocks(zr.at[q], N_NODE - 1, z_recv.at[q])
-        wide = jnp.concatenate([zr[q, :, s, :] for s in range(8)], axis=1)
+        wait_blocks(landed(q), N_NODE - 1, z_recv.at[q])
+        if q == LAST:
+            wide = jnp.concatenate([zr_last[:, s, :] for s in range(4)], axis=1)
+        else:
+            wide = jnp.concatenate([zr[q, :, s, :] for s in range(8)], axis=1)
         gram[:, :N_NODE] += lax.dot_general(
             wide, wide, (((1,), (1,)), ((), ())), precision=lax.Precision.HIGHEST, preferred_element_type=F32
         )
 
-    for step in range(NQ + 4):
-        if step < NQ:
-            stage1(step)
-            stage2(step)
-        if 0 <= step - 2 < NQ:
-            stage4(step - 2)
-        if 0 <= step - 1 < NQ:
-            stage3(step - 1)
-        if 0 <= step - 3 < NQ:
-            stage5(step - 3)
-        if 0 <= step - 4 < NQ:
-            stage6(step - 4)
+    def when(stage, q):
+        if 0 <= q < NQ:
+            stage(q)
+
+    for step in range(NQ + 3):
+        when(stage1, step)
+        when(stage5, step - 2)
+        when(stage1_rest, step)
+        when(stage3, step - 1)
+        when(stage1_send, step)
+        when(stage2, step)
+        when(stage4, step - 1)
+        when(stage6, step - 3)
 
     def exchange(n, value, buf, count, slot, peer):
         sb[n] = value
@@ -310,21 +355,27 @@
     spread = jnp.broadcast_to(coefs, (N_NODE, 128))
     merged = []
     for q in range(NQ):
-        total = spread[0:1, :] * zr[q, 0]
+        blocks = landed(q)
+        total = spread[0:1, :] * blocks[0]
         for n in range(1, N_NODE):
-            total = total + spread[n : n + 1, :] * zr[q, n]
+            total = total + spread[n : n + 1, :] * blocks[n]
         merged.append(total)
     for a in range(2):
-        for q in range(NQ):
+        for q in range(LAST):
             first, m = CHUNKS[q]
             out_ref[8 * a : 8 * a + 8, first : first + m] = merged[q][:, 64 * a : 64 * a + m]
+        first, m = CHUNKS[LAST]
+        for b in range(2):
+            row0, lane0 = 8 * a + 4 * b, 64 * b + m * a
+            out_ref[row0 : row0 + 4, first : first + m] = merged[LAST][:, lane0 : lane0 + m]
 
     for q in range(NQ):
         for h in range(2):
             for kind in range(6):
                 p1_copy(q, h, kind).wait_send()
+            for kind in range(P2_KINDS[q]):
                 p2_copy(q, h, kind).wait_send()
-        wait_blocks(zr.at[q], N_NODE - 1, z_send.at[q])
+        wait_blocks(landed(q), N_NODE - 1, z_send.at[q])
     for n, (buf, count) in enumerate(((s1, 8), (s2, 4), (s3, N_LOCAL))):
         wait_blocks(buf, count - 1, s_send.at[n])
 
@@ -344,7 +395,8 @@
             vmem((TAPS * C, C), BF16), vmem((TAPS * C, C), BF16),
             vmem((OUT_ROWS, C), F32), vmem((C, C), BF16), vmem((C, C), BF16),
             vmem((2, 16 * ROWS_L, HALF), F32), vmem((2, 12 * ROWS_L, HALF), F32), vmem((2, 3 * ROWS_L, HALF), F32),
-            vmem((NQ, HALF, 128), F32), vmem((NQ, N_NODE, 8, 128), F32),
+            vmem((LAST, HALF, 128), F32), vmem((LAST, N_NODE, 8, 128), F32),
+            vmem((N_NODE, 4, 128), F32), vmem((N_NODE, 4, 128), F32),
             vmem((N_NODE, 128), F32), vmem((3, 8, 128), F32),
             vmem((8, 8, 128), F32), vmem((4, 8, 128), F32), vmem((N_LOCAL, 8, 128), F32),
             dma((2 + TAPS,)), dma((12 * NQ,)), dma((12 * NQ,)), dma((12 * NQ,)), dma((12 * NQ,)),

time: 115 us -> 105 us (0.913)
  Pallas kernels: 113 us -> 104 us
    pallas_call x1, Pallas kernels: 113 us -> 104 us  [on_device(): pl.pallas_call(kernel, out_shape=jax.ShapeDtypeStruct((C // N_NODE, ROWS_...]
where the time goes in v3:
time: 105 us
  Pallas kernels  104 us (99%)
  local copies, waits for them, and re-layouts  1.35 us (1%)
    pallas_call x1, Pallas kernels, on_device(): pl.pallas_call(kernel, out_shape=jax.ShapeDtypeStruct((C // N_NODE, ROWS_...  104 us

profile of v3, /device:TPU:1, one launch (start us, length us, event | category | flops | bytes accessed | tf_op | source)
XLA Modules:
  0.0 104.9 jit_solution(15983244569598813583)
XLA Ops:
  0.0 103.5 %shard_map.37 = f32[16,288]{1,0:T(8,128)} custom-call(f32[7,7,8,512]{3,2,1,0:T(8,128)} %bitcast.6, f32[7,7,8,512]{3,2,1,0:T(8,128)} %bitcast.7, f32[9,512,512]{2,1,0:T(8,128)} %bitcast.5), custom_call_target="tpu_custom_call" | custom-call | flops 12000000000 | bytes 12000000 | tf_op jit(solution)/shard_map/pallas_call | solution.py:387
  103.5 1.3 %copy.5 = f32[288,16]{0,1:T(8,128)} copy(f32[288,16]{0,1:T(8,128)} %bitcast.4) | data formatting | bytes 36864

commit v4 on v3

--- a/solution.py
+++ b/solution.py
@@ -17,7 +17,7 @@
 CHUNKS = ((0, 64), (64, 64), (128, 64), (192, 64), (256, 32))
 NQ = len(CHUNKS)
 LAST = NQ - 1
-P2_KINDS = (6, 6, 6, 6, 3)
+DIRECT = LAST - 1
 BASE = (0, 64, 128, 192, 256)
 MESH = pl.DeviceIdType.MESH
 
@@ -132,7 +132,7 @@
 
     def p2_slot(q, h, kind):
         m = CHUNKS[q][1]
-        if q == LAST:
+        if q >= DIRECT:
             return p2.at[h, 3 * BASE[q] + kind * m : 3 * BASE[q] + (kind + 1) * m, :]
         first = 3 * BASE[q] + kind * (m // 2)
         return p2.at[h, first : first + m // 2, :]
@@ -150,7 +150,7 @@
 
     def p2_copy(q, h, kind):
         n = (q * 2 + h) * 6 + kind
-        if q == LAST:
+        if q >= DIRECT:
             src, hop = block(q, h, 0, (1, 3, 2)[kind], (1, 3, 2)[kind] + 1), kind
         else:
             src, hop = kept(q, h, *P2_PART[kind]), kind % 2
@@ -204,7 +204,7 @@
             for kind in (2, 3, 4, 5):
                 p1_copy(q, h, kind).wait_recv()
             block(q, h, 0, 2, 4)[...] += p1_slot(q, h, 2)[...] + p1_slot(q, h, 5)[...]
-            if q == LAST:
+            if q >= DIRECT:
                 block(q, h, 0, 0, 2)[...] += p1_slot(q, h, 3)[...] + p1_slot(q, h, 4)[...]
                 for kind in (2, 0, 1):
                     p2_copy(q, h, kind).start()
@@ -216,7 +216,7 @@
             p2_copy(q, h, 3).start()
 
     def stage4(q):
-        if q == LAST:
+        if q >= DIRECT:
             return
         for h in range(2):
             for side in range(2):
@@ -238,7 +238,7 @@
         m = CHUNKS[q][1]
         parts = []
         for h in range(2):
-            if q == LAST:
+            if q >= DIRECT:
                 for kind in (0, 1, 2):
                     p2_copy(q, h, kind).wait_recv()
                 parts.append(
@@ -288,7 +288,7 @@
         if 0 <= q < NQ:
             stage(q)
 
-    for step in range(NQ + 3):
+    for step in range(NQ):
         when(stage1, step)
         when(stage5, step - 2)
         when(stage1_rest, step)
@@ -297,6 +297,12 @@
         when(stage2, step)
         when(stage4, step - 1)
         when(stage6, step - 3)
+    stage5(LAST - 1)
+    stage3(LAST)
+    stage6(LAST - 2)
+    stage5(LAST)
+    stage6(LAST - 1)
+    stage6(LAST)
 
     def exchange(n, value, buf, count, slot, peer):
         sb[n] = value
@@ -373,7 +379,7 @@
         for h in range(2):
             for kind in range(6):
                 p1_copy(q, h, kind).wait_send()
-            for kind in range(P2_KINDS[q]):
+            for kind in range(3 if q >= DIRECT else 6):
                 p2_copy(q, h, kind).wait_send()
         wait_blocks(landed(q), N_NODE - 1, z_send.at[q])
     for n, (buf, count) in enumerate(((s1, 8), (s2, 4), (s3, N_LOCAL))):

time: 105 us -> 105 us (level)
  no operation moved by 1% of the time
where the time goes in v4:
time: 105 us
  Pallas kernels  103 us (98%)
  local copies, waits for them, and re-layouts  1.35 us (1%)
    pallas_call x1, Pallas kernels, on_device(): pl.pallas_call(kernel, out_shape=jax.ShapeDtypeStruct((C // N_NODE, ROWS_...  103 us

profile of v4, /device:TPU:1, one launch (start us, length us, event | category | flops | bytes accessed | tf_op | source)
XLA Modules:
  0.0 104.5 jit_solution(17334263795471699438)
XLA Ops:
  0.0 103.2 %shard_map.37 = f32[16,288]{1,0:T(8,128)} custom-call(f32[7,7,8,512]{3,2,1,0:T(8,128)} %bitcast.6, f32[7,7,8,512]{3,2,1,0:T(8,128)} %bitcast.7, f32[9,512,512]{2,1,0:T(8,128)} %bitcast.5), custom_call_target="tpu_custom_call" | custom-call | flops 12000000000 | bytes 12000000 | tf_op jit(solution)/shard_map/pallas_call | solution.py:393
  103.2 1.3 %copy.5 = f32[288,16]{0,1:T(8,128)} copy(f32[288,16]{0,1:T(8,128)} %bitcast.4) | data formatting | bytes 36864

commit v5 on v4

--- a/solution.py
+++ b/solution.py
@@ -257,7 +257,7 @@
         else:
             zs[q] = jnp.concatenate(parts, axis=0).T
 
-        @pl.loop(0, N_NODE - 1)
+        @pl.loop(0, N_NODE - 1, unroll=q == LAST)
         def _(k):
             far = N_NODE // 2 + jnp.where(lax.rem(k, 2) == 1, (k + 1) // 2, -((k + 1) // 2))
             z_copy(q, lax.rem(node + far, N_NODE)).start()
@@ -299,8 +299,8 @@
         when(stage6, step - 3)
     stage5(LAST - 1)
     stage3(LAST)
+    stage5(LAST)
     stage6(LAST - 2)
-    stage5(LAST)
     stage6(LAST - 1)
     stage6(LAST)
 
@@ -308,8 +308,8 @@
         sb[n] = value
         buf[slot] = value
 
-        @pl.loop(1, count)
-        def _(d):
+        for k in range(1, count):
+            d = count // 2 + (k // 2 if k % 2 else -(k // 2))
             pltpu.make_async_remote_copy(
                 src_ref=sb.at[n], dst_ref=buf.at[slot], send_sem=s_send.at[n], recv_sem=s_recv.at[n],
                 device_id=peer(d), device_id_type=MESH,

time: 105 us -> 104 us (level)
  no operation moved by 1% of the time
where the time goes in v5:
time: 104 us
  Pallas kernels  103 us (99%)
  local copies, waits for them, and re-layouts  1.35 us (1%)
    pallas_call x1, Pallas kernels, on_device(): pl.pallas_call(kernel, out_shape=jax.ShapeDtypeStruct((C // N_NODE, ROWS_...  103 us

profile of v5, /device:TPU:1, one launch (start us, length us, event | category | flops | bytes accessed | tf_op | source)
XLA Modules:
  0.0 104.3 jit_solution(18032113565123541626)
XLA Ops:
  0.0 102.9 %shard_map.37 = f32[16,288]{1,0:T(8,128)} custom-call(f32[7,7,8,512]{3,2,1,0:T(8,128)} %bitcast.6, f32[7,7,8,512]{3,2,1,0:T(8,128)} %bitcast.7, f32[9,512,512]{2,1,0:T(8,128)} %bitcast.5), custom_call_target="tpu_custom_call" | custom-call | flops 12000000000 | bytes 12000000 | tf_op jit(solution)/shard_map/pallas_call | solution.py:393
  102.9 1.3 %copy.5 = f32[288,16]{0,1:T(8,128)} copy(f32[288,16]{0,1:T(8,128)} %bitcast.4) | data formatting | bytes 36864

commit v6 on v5

--- a/solution.py
+++ b/solution.py
@@ -31,6 +31,10 @@
     return jnp.dot(a, b, preferred_element_type=F32)
 
 
+def dot3(a_hi, a_lo, b_hi, b_lo):
+    return dot(jnp.concatenate([a_hi, a_hi, a_lo], axis=1), jnp.concatenate([b_hi, b_lo, b_hi], axis=0))
+
+
 def kernel(
     x_hbm, t_hbm, w_hbm, out_ref,
     xin, tin, wbuf, xs_hi, xs_lo, xt_hi, xt_lo, acc, r_hi, r_lo, g, p1, p2, zs, zr, zs_last, zr_last, gram, sb, s1, s2, s3,
@@ -94,7 +98,7 @@
             w_hi, w_lo = split(wbuf[t])
             x_hi = xs_hi[pl.ds(start, OUT_ROWS), :]
             x_lo = xs_lo[pl.ds(start, OUT_ROWS), :]
-            total = total + (dot(x_hi, w_hi) + dot(x_hi, w_lo) + dot(x_lo, w_hi))
+            total = total + dot3(x_hi, x_lo, w_hi, w_lo)
             rows = pl.ds(pl.multiple_of(t * C, C), C)
             xt_hi[rows, :] = xs_hi[pl.ds(start, C), :].T
             xt_lo[rows, :] = xs_lo[pl.ds(start, C), :].T
@@ -172,7 +176,7 @@
         a_lo = jnp.concatenate(parts_lo, axis=0)
         cols = slice(h * HALF, (h + 1) * HALF)
         b_hi, b_lo = r_hi[:, cols], r_lo[:, cols]
-        block(q, h, i, 0, 4)[...] = dot(a_hi, b_hi) + dot(a_hi, b_lo) + dot(a_lo, b_hi)
+        block(q, h, i, 0, 4)[...] = dot3(a_hi, a_lo, b_hi, b_lo)
 
     def stage1(q):
         for h in range(2):

time: 104 us -> 104 us (level)
  no operation moved by 1% of the time
where the time goes in v6:
time: 104 us
  Pallas kernels  103 us (99%)
  local copies, waits for them, and re-layouts  1.35 us (1%)
    pallas_call x1, Pallas kernels, on_device(): pl.pallas_call(kernel, out_shape=jax.ShapeDtypeStruct((C // N_NODE, ROWS_...  103 us

profile of v6, /device:TPU:1, one launch (start us, length us, event | category | flops | bytes accessed | tf_op | source)
XLA Modules:
  0.0 103.9 jit_solution(13050688205229259427)
XLA Ops:
  0.0 102.6 %shard_map.37 = f32[16,288]{1,0:T(8,128)} custom-call(f32[7,7,8,512]{3,2,1,0:T(8,128)} %bitcast.6, f32[7,7,8,512]{3,2,1,0:T(8,128)} %bitcast.7, f32[9,512,512]{2,1,0:T(8,128)} %bitcast.5), custom_call_target="tpu_custom_call" | custom-call | flops 12000000000 | bytes 12000000 | tf_op jit(solution)/shard_map/pallas_call | solution.py:397
  102.6 1.3 %copy.5 = f32[288,16]{0,1:T(8,128)} copy(f32[288,16]{0,1:T(8,128)} %bitcast.4) | data formatting | bytes 36864
